TPU v7x, 32 devices: a whole 2x2x4 slice. The times are simulated.
32 devices in a mesh: shard: 8 (over z, x), tensor: 4 (over y, core).
Axes of the slice: x: 2, y: 2, z: 4, core: 2. Of those that a mesh axis runs over, the one named last changes fastest.
Arguments:
- grads: bfloat16 [8, 4, 1536, 1024], P('shard', None, None, 'tensor'), may hold values from -240 to 240
- master: float32 [1536, 1024], P('shard', 'tensor'), may hold values from -3 to 3
- moment1: float32 [1536, 1024], P('shard', 'tensor'), may hold values from -3 to 3
- moment2: float32 [1536, 1024], P('shard', 'tensor'), may hold values from 0.25 to 1
- ema: float32 [1536, 1024], P('shard', 'tensor'), may hold values from -3 to 3
Outputs:
- new_master: float32 [1536, 1024], P('shard', 'tensor')
- new_moment1: float32 [1536, 1024], P('shard', 'tensor')
- new_moment2: float32 [1536, 1024], P('shard', 'tensor')
- new_ema: float32 [1536, 1024], P('shard', 'tensor')
- weights: bfloat16 [1536, 1024], P(None, 'tensor')
All inputs are finite; a program needn't handle non-finite values.
Results may differ from a plain program's by a relative error of at most 0.0004.
Values may be sent and summed in bfloat16 or wider, within the bound.
A program may use at most 64 MiB of HBM per device.

v0:
```python
import jax
import jax.numpy as jnp
from jax import lax
from jax.sharding import PartitionSpec as P

STEP = 10


beta_one = 0.9
beta_two = 0.95
learn_rate = 0.02
decay_weight = 0.1
ema_keep = 0.99


def shards(grads, master, moment1, moment2, ema):
    local = grads[0]
    elements = local.shape[1] * local.shape[2] * lax.axis_size("tensor")
    summed = jnp.sum(local.astype(jnp.float32), axis=0)
    grad_part = lax.psum_scatter(summed, "shard", scatter_dimension=0, tiled=True)
    sq = lax.psum(jnp.sum(grad_part * grad_part), ("shard", "tensor"))
    scale = jnp.minimum(1.0, 1.0 / jnp.sqrt(sq / elements + 1e-06))
    clipped = scale * grad_part
    new_moment1 = beta_one * moment1 + (1.0 - beta_one) * clipped
    new_moment2 = beta_two * moment2 + (1.0 - beta_two) * clipped * clipped
    first_hat = new_moment1 / (1.0 - beta_one**STEP)
    second_hat = new_moment2 / (1.0 - beta_two**STEP)
    new_master = master - learn_rate * (
        first_hat / (jnp.sqrt(second_hat) + 1e-08) + decay_weight * master
    )
    new_ema = ema_keep * ema + (1.0 - ema_keep) * new_master
    weights = lax.all_gather(new_master.astype(jnp.bfloat16), "shard", axis=0, tiled=True)
    return (new_master, new_moment1, new_moment2, new_ema, weights)


def solution(mesh):
    return jax.shard_map(
        shards,
        mesh=mesh,
        in_specs=(
            P("shard", None, None, "tensor"),
            P("shard", "tensor"),
            P("shard", "tensor"),
            P("shard", "tensor"),
            P("shard", "tensor"),
        ),
        out_specs=(
            P("shard", "tensor"),
            P("shard", "tensor"),
            P("shard", "tensor"),
            P("shard", "tensor"),
            P(None, "tensor"),
        ),
        check_vma=False,
    )
```

profile of v0, /device:TPU:0, one launch (start us, length us, event | category | flops | bytes accessed | tf_op | source)
XLA Modules:
  0.0 163.5 jit_solution(3003033141278856340)
XLA Ops:
  7.2 0.0 copy-start.4
  7.2 0.0 copy-start.3
  7.2 0.0 copy-start.2
  7.2 0.0 reduce-scatter.2.cloned.1.call-start
  7.2 3.7 %convert_reduce_fusion = f32[1536,256]{1,0:T(8,128)} fusion(bf16[1,4,1536,256]{3,2,1,0:T(8,128)(2,1)} %param.5), kind=kLoop, calls=%fused_computation | loop fusion | flops 2752512 | bytes 4718592 | tf_op jit(solution)/shard_map/reduce_sum | solution.py:19
  11.0 0.0 copy-start.1
  11.0 0.0 reduce-scatter.2.cloned.1.call-update
  11.0 67.9 %reduce-scatter.2.cloned.1.call-done = f32[192,256]{1,0:T(8,128)} async-done(((f32[1536,256]{1,0:T(8,128)}), f32[192,256]{1,0:T(8,128)}) %reduce-scatter.2.cloned.1.call-update) | async-done | bytes 196624 | tf_op jit(solution)/shard_map/reduce_scatter | solution.py:20
  79.0 1.6 multiply_reduce_fusion
  80.5 39.9 %psum.7 = f32[]{:T(128)} all-reduce(f32[]{:T(128)} %multiply_reduce_fusion), channel_id=1, replica_groups=mesh['shard'=8,'tensor'=4] {'shard','tensor'}, use_global_device_ids=true, to_apply=%region_3.0 | all-reduce | flops 1 | bytes 8 | tf_op jit(solution)/shard_map/psum | solution.py:21
  121.2 0.0 copy-done.4
  121.2 0.0 copy-done.3
  121.2 0.0 copy-done.2
  121.2 1.8 %fusion.1 = (bf16[192,256]{1,0:T(8,128)(2,1)S(1)}, f32[192,256]{1,0:T(8,128)S(1)}, f32[192,256]{1,0:T(8,128)}, f32[192,256]{1,0:T(8,128)}) fusion(f32[192,256]{1,0:T(8,128)S(1)} %copy-done.2, f32[192,256]{1,0:T(8,128)} %reduce-scatter.2.cloned.1.call-done, f32[]{:T(128)S(6)} %min.3, f32[192,256]{1,0:T(8,128)S(1)} %copy-done.3, f32[192,256]{1,0:T(8,128)S(1)} %copy-done.4), kind=kLoop, calls=%fused_computation.7 | loop fusion | flops 835584 | bytes 1474564 | tf_op jit(solution)/shard_map/convert_element_type | solution.py:32
  123.0 0.0 copy-start
  123.0 32.0 %all_gather.3 = bf16[1536,256]{1,0:T(8,128)(2,1)S(1)} all-gather(bf16[192,256]{1,0:T(8,128)(2,1)S(1)} %get-tuple-element.5), channel_id=1, replica_groups=mesh['shard'=8,'tensor'=4] {'shard'}, dimensions={0}, use_global_device_ids=true | all-gather | bytes 884736 | tf_op jit(solution)/shard_map/all_gather | solution.py:32
  155.0 0.0 copy-done.1
  155.0 0.7 multiply_add_fusion
  155.7 0.9 copy.11
  156.6 0.0 copy-done
Async XLA Ops:
  7.2 114.0 %copy-start.4 = (f32[192,256]{1,0:T(8,128)S(1)}, f32[192,256]{1,0:T(8,128)}, u32[]{:S(2)}) copy-start(f32[192,256]{1,0:T(8,128)} %param.8) | copy-start | bytes 589828
  7.2 114.0 %copy-start.3 = (f32[192,256]{1,0:T(8,128)S(1)}, f32[192,256]{1,0:T(8,128)}, u32[]{:S(2)}) copy-start(f32[192,256]{1,0:T(8,128)} %param.7) | copy-start | bytes 589828
  7.2 114.0 %copy-start.2 = (f32[192,256]{1,0:T(8,128)S(1)}, f32[192,256]{1,0:T(8,128)}, u32[]{:S(2)}) copy-start(f32[192,256]{1,0:T(8,128)} %param.6) | copy-start | bytes 589828
  7.2 71.8 %reduce-scatter.2.cloned.1.call-start = ((), (), s32[]{:S(2)}) async-start(), calls=%async_computation.1 | async-start | bytes 1769472 | tf_op jit(solution)/shard_map/reduce_scatter | solution.py:20
  11.0 144.0 %copy-start.1 = (f32[192,256]{1,0:T(8,128)S(1)}, f32[192,256]{1,0:T(8,128)}, u32[]{:S(2)}) copy-start(f32[192,256]{1,0:T(8,128)} %param.9) | copy-start | bytes 589828
  123.0 33.6 %copy-start = (f32[192,256]{1,0:T(8,128)}, f32[192,256]{1,0:T(8,128)S(1)}, u32[]{:S(2)}) copy-start(f32[192,256]{1,0:T(8,128)S(1)} %get-tuple-element.14) | copy-start | bytes 589828
Sparse Core Ops, SparseCore 0:
  11.4 67.4 reduce-scatter.1
where the time goes:
time: 164 us; the launch traced here: 163 us
  blocking collectives  71.9 us (44%)
  waiting for transfers between devices  68 us (41%)
  between operations  14.8 us (9%)
  other arithmetic  7.86 us (5%)
    reduce_scatter x1, waiting for transfers between devices, shards(): lax.psum_scatter(summed, 'shard', scatter_dimension=0, tiled=True)  67.9 us
    psum x1, blocking collectives, shards(): sq = lax.psum(jnp.sum(grad_part * grad_part), ('shard', 'tensor'))  39.9 us
    all_gather x1, blocking collectives, shards(): lax.all_gather(new_master.astype(jnp.bfloat16), 'shard', axis=0, tiled=True)  32 us
    reduce_sum x1, other arithmetic, shards(): summed = jnp.sum(local.astype(jnp.float32), axis=0)  3.75 us
  transfers between devices with their start and end apart: 1, of which 1 were waited for; matrix products, arithmetic and copies ran while one was open for 0% of the time, Pallas kernels for 0%

commit v1 on v0

--- a/solution.py
+++ b/solution.py
@@ -1,10 +1,11 @@
 import jax
 import jax.numpy as jnp
 from jax import lax
+from jax.experimental import pallas as pl
+from jax.experimental.pallas import tpu as pltpu
 from jax.sharding import PartitionSpec as P
 
 STEP = 10
-
 
 beta_one = 0.9
 beta_two = 0.95
@@ -12,8 +13,30 @@
 decay_weight = 0.1
 ema_keep = 0.99
 
-
-def shards(grads, master, moment1, moment2, ema):
+MESH = pl.DeviceIdType.MESH
+TILE = 32
+
+GAIN = 16.0
+LINEAR = 2.0**-12
+
+
+def encode(value):
+    u = jnp.abs(value) * GAIN
+    u2 = u * u
+    u4 = u2 * u2
+    power = jnp.where(u < LINEAR, u * LINEAR**7, u4 * u4)
+    return jnp.where(value < 0, -power, power).astype(jnp.bfloat16)
+
+
+def decode(code):
+    y = code.astype(jnp.float32)
+    a = jnp.abs(y)
+    fourth = lax.rsqrt(lax.rsqrt(a))
+    root = jnp.where(a < LINEAR**8, a * (LINEAR**-7 / GAIN), fourth * lax.rsqrt(fourth) * (1.0 / GAIN))
+    return jnp.where(y < 0, -root, root)
+
+
+def plain(grads, master, moment1, moment2, ema):
     local = grads[0]
     elements = local.shape[1] * local.shape[2] * lax.axis_size("tensor")
     summed = jnp.sum(local.astype(jnp.float32), axis=0)
@@ -33,7 +56,268 @@
     return (new_master, new_moment1, new_moment2, new_ema, weights)
 
 
+def make_kernel(n_tensor, micro, rows, cols):
+    n_shard = 8
+    elements = n_shard * rows * cols * n_tensor
+
+    def kernel(g, ma, m1, m2, em, o_ma, o_m1, o_m2, o_em, o_w,
+               gv, st, out, part, sx, rx, sz, rz, w, sq_a, sq_b,
+               load_sem, store_sem, send_sem, recv_sem, sqs_sem, sqr_sem):
+        s = lax.axis_index("shard")
+        t = lax.axis_index("tensor")
+        x = lax.rem(s, 2)
+        z = s // 2
+        other = 1 - x
+        zs = (z, z + 1 - 2 * lax.rem(z, 2), lax.rem(z + 2, 4), 3 - z)
+        to_x = {"shard": 2 * z + other}
+        to_z = {1: {"shard": 2 * zs[1] + x}, 2: {"shard": 2 * zs[2] + x}}
+        order = (3, 2, 1, 0)
+
+        def block(j, xx):
+            return pl.ds(pl.multiple_of((2 * zs[j] + xx) * rows, rows), rows)
+
+        loads = {}
+        for i, (j, mine) in enumerate([(j, False) for j in order] + [(j, True) for j in order]):
+            loads[j, mine] = (i, pltpu.make_async_copy(
+                g.at[0, :, block(j, x if mine else other), :], gv.at[i], load_sem.at[i]))
+            loads[j, mine][1].start()
+        state = []
+        for i, ref in enumerate((ma, m1, m2, em)):
+            state.append(pltpu.make_async_copy(ref, st.at[i], load_sem.at[8 + i]))
+            state[-1].start()
+
+        barrier = pltpu.get_barrier_semaphore()
+        for k in range(1, n_shard):
+            pl.semaphore_signal(barrier, inc=1, device_id={"shard": lax.rem(s + k, n_shard)}, device_id_type=MESH)
+        for k in range(1, n_tensor):
+            pl.semaphore_signal(barrier, inc=1, device_id={"tensor": lax.rem(t + k, n_tensor)}, device_id_type=MESH)
+
+        def tiles(body, init=0):
+            def step(i, carry):
+                return body(pl.ds(pl.multiple_of(i * TILE, TILE), TILE), carry)
+            return lax.fori_loop(0, rows // TILE, step, init)
+
+        def micro_sum(slot, r):
+            total = gv[slot, 0, r, :].astype(jnp.float32)
+            for m in range(1, micro):
+                total = total + gv[slot, m, r, :].astype(jnp.float32)
+            return total
+
+        sent = []
+
+        def send(src, dst, index, target):
+            copy = pltpu.make_async_remote_copy(
+                src_ref=src, dst_ref=dst, send_sem=send_sem.at[index], recv_sem=recv_sem.at[index],
+                device_id=target, device_id_type=MESH)
+            copy.start()
+            sent.append(copy)
+            return copy
+
+        over_x = {}
+        for n, j in enumerate(order):
+            slot, copy = loads[j, False]
+            copy.wait()
+
+            def body(r, c, slot=slot, j=j):
+                sx[j, r, :] = encode(micro_sum(slot, r))
+                return c
+            tiles(body)
+            if n == 0:
+                pl.semaphore_wait(barrier, n_shard - 1 + n_tensor - 1)
+            over_x[j] = send(sx.at[j], rx.at[j], j, to_x)
+
+        for j in order:
+            slot, copy = loads[j, True]
+            copy.wait()
+
+            def body(r, c, slot=slot, j=j):
+                part[j, r, :] = micro_sum(slot, r)
+                return c
+            tiles(body)
+
+        over_x[3].wait_recv()
+
+        def body(r, c):
+            sz[0, r, :] = encode(part[3, r, :] + decode(rx[3, r, :]))
+            return c
+        tiles(body)
+        first = send(sz.at[0], rz.at[0], 4, to_z[1])
+
+        over_x[2].wait_recv()
+        first.wait_recv()
+
+        def body(r, c):
+            sz[1, r, :] = encode(part[2, r, :] + decode(rx[2, r, :]) + decode(rz[0, r, :]))
+            return c
+        tiles(body)
+        far = send(sz.at[1], rz.at[1], 5, to_z[2])
+
+        over_x[1].wait_recv()
+
+        def body(r, c):
+            sz[2, r, :] = encode(part[1, r, :] + decode(rx[1, r, :]))
+            return c
+        tiles(body)
+        near = send(sz.at[2], rz.at[2], 6, to_z[1])
+
+        over_x[0].wait_recv()
+
+        def body(r, c):
+            part[0, r, :] = part[0, r, :] + decode(rx[0, r, :])
+            return c
+        tiles(body)
+        near.wait_recv()
+
+        def body(r, c):
+            part[0, r, :] = part[0, r, :] + decode(rz[2, r, :])
+            return c
+        tiles(body)
+        far.wait_recv()
+
+        def body(r, acc):
+            total = part[0, r, :] + decode(rz[1, r, :])
+            part[0, r, :] = total
+            square = total * total
+            square = square[:, :cols // 2] + square[:, cols // 2:]
+            return acc + jnp.sum(square.reshape(TILE // 8, 8, cols // 2), axis=0)
+        acc = tiles(body, jnp.zeros((8, cols // 2), jnp.float32))
+
+        def gather(buffer, axis, me, count, base):
+            copies = []
+            for k in range(1, count):
+                copies.append(pltpu.make_async_remote_copy(
+                    src_ref=buffer.at[me], dst_ref=buffer.at[me],
+                    send_sem=sqs_sem.at[base + k], recv_sem=sqr_sem.at[base + k],
+                    device_id={axis: lax.rem(me + k, count)}, device_id_type=MESH))
+                copies[-1].start()
+            for copy in copies:
+                copy.wait_recv()
+            sent.extend(copies)
+            total = buffer[0]
+            for i in range(1, count):
+                total = total + buffer[i]
+            return total
+
+        sq_a[s] = jnp.sum(acc, axis=0, keepdims=True)
+        sq_b[t] = gather(sq_a, "shard", s, n_shard, 0)
+        sq = jnp.sum(gather(sq_b, "tensor", t, n_tensor, n_shard), axis=1, keepdims=True)
+        scale = jnp.minimum(1.0, 1.0 / jnp.sqrt(sq / elements + 1e-06))
+
+        for copy in state:
+            copy.wait()
+
+        def body(r, c):
+            clipped = scale * part[0, r, :]
+            new_m1 = beta_one * st[1, r, :] + (1.0 - beta_one) * clipped
+            new_m2 = beta_two * st[2, r, :] + (1.0 - beta_two) * clipped * clipped
+            first_hat = new_m1 / (1.0 - beta_one**STEP)
+            second_hat = new_m2 / (1.0 - beta_two**STEP)
+            old = st[0, r, :]
+            new_ma = old - learn_rate * (first_hat / (jnp.sqrt(second_hat) + 1e-08) + decay_weight * old)
+            w[s, r, :] = new_ma.astype(jnp.bfloat16)
+            out[0, r, :] = new_ma
+            out[1, r, :] = new_m1
+            out[2, r, :] = new_m2
+            return c
+        tiles(body)
+
+        def gathered(slot, index, target):
+            return send(w.at[slot], w.at[slot], index, target)
+
+        slot_x = [2 * zj + x for zj in zs]
+        slot_o = [2 * zj + other for zj in zs]
+        far = gathered(s, 9, to_z[2])
+        near = gathered(s, 8, to_z[1])
+        side = gathered(s, 7, to_x)
+
+        stores = []
+
+        def store(src, dst):
+            copy = pltpu.make_async_copy(src, dst, store_sem.at[len(stores)])
+            copy.start()
+            stores.append(copy)
+
+        def store_w(slot):
+            store(w.at[slot], o_w.at[pl.ds(pl.multiple_of(slot * rows, rows), rows), :])
+
+        store(out.at[0], o_ma)
+        store(out.at[1], o_m1)
+        store(out.at[2], o_m2)
+        store_w(s)
+
+        def body(r, c):
+            out[3, r, :] = ema_keep * st[3, r, :] + (1.0 - ema_keep) * out[0, r, :]
+            return c
+        tiles(body)
+        store(out.at[3], o_em)
+
+        near.wait_recv()
+        side_1 = gathered(slot_x[1], 11, to_x)
+        store_w(slot_x[1])
+        far.wait_recv()
+        near_2 = gathered(slot_x[2], 10, to_z[1])
+        side_2 = gathered(slot_x[2], 12, to_x)
+        store_w(slot_x[2])
+        side.wait_recv()
+        store_w(slot_o[0])
+        near_2.wait_recv()
+        side_3 = gathered(slot_x[3], 13, to_x)
+        store_w(slot_x[3])
+        for copy, j in ((side_1, 1), (side_2, 2), (side_3, 3)):
+            copy.wait_recv()
+            store_w(slot_o[j])
+        for copy in sent:
+            copy.wait_send()
+        for copy in stores:
+            copy.wait()
+
+    return kernel
+
+
+def fused(grads, master, moment1, moment2, ema):
+    n_tensor = lax.axis_size("tensor")
+    micro = grads.shape[1]
+    rows, cols = master.shape
+    f32 = jax.ShapeDtypeStruct((rows, cols), jnp.float32)
+    full = jax.ShapeDtypeStruct((8 * rows, cols), jnp.bfloat16)
+    hbm = pl.BlockSpec(memory_space=pl.ANY)
+    return pl.pallas_call(
+        make_kernel(n_tensor, micro, rows, cols),
+        out_shape=(f32, f32, f32, f32, full),
+        in_specs=[hbm] * 5,
+        out_specs=(hbm,) * 5,
+        scratch_shapes=[
+            pltpu.VMEM((8, micro, rows, cols), jnp.bfloat16),
+            pltpu.VMEM((4, rows, cols), jnp.float32),
+            pltpu.VMEM((4, rows, cols), jnp.float32),
+            pltpu.VMEM((4, rows, cols), jnp.float32),
+            pltpu.VMEM((4, rows, cols), jnp.bfloat16),
+            pltpu.VMEM((4, rows, cols), jnp.bfloat16),
+            pltpu.VMEM((3, rows, cols), jnp.bfloat16),
+            pltpu.VMEM((3, rows, cols), jnp.bfloat16),
+            pltpu.VMEM((8, rows, cols), jnp.bfloat16),
+            pltpu.VMEM((8, 1, cols // 2), jnp.float32),
+            pltpu.VMEM((n_tensor, 1, cols // 2), jnp.float32),
+            pltpu.SemaphoreType.DMA((12,)),
+            pltpu.SemaphoreType.DMA((12,)),
+            pltpu.SemaphoreType.DMA((14,)),
+            pltpu.SemaphoreType.DMA((14,)),
+            pltpu.SemaphoreType.DMA((8 + n_tensor,)),
+            pltpu.SemaphoreType.DMA((8 + n_tensor,)),
+        ],
+        compiler_params=pltpu.CompilerParams(
+            collective_id=0, has_side_effects=True, vmem_limit_bytes=32 * 1024 * 1024
+        ),
+        cost_estimate=pl.CostEstimate(flops=20_000_000, bytes_accessed=6_000_000, transcendentals=300_000),
+    )(grads, master, moment1, moment2, ema)
+
+
 def solution(mesh):
+    def shards(grads, master, moment1, moment2, ema):
+        if mesh.shape["shard"] == 8 and master.shape[0] % TILE == 0 and master.shape[1] == 256:
+            return fused(grads, master, moment1, moment2, ema)
+        return plain(grads, master, moment1, moment2, ema)
+
     return jax.shard_map(
         shards,
         mesh=mesh,

time: 164 us -> 53.8 us (0.33)
  blocking collectives: 71.9 us -> 0 us
  waiting for transfers between devices: 68 us -> 0 us
  Pallas kernels: 0 us -> 43.7 us
  between operations: 14.8 us -> 0.66 us
  local copies, waits for them, and re-layouts: 0.9 us -> 9.18 us
  other arithmetic: 7.86 us -> 0 us
    reduce_scatter x1 -> x0, waiting for transfers between devices: 67.9 us -> none  [shards(): lax.psum_scatter(summed, 'shard', scatter_dimension=0, tiled=True)]
    pallas_call x0 -> x1, Pallas kernels: none -> 43.7 us  [fused(): pl.pallas_call(make_kernel(n_tensor, micro, rows, cols), out_shape=(f32,...]
    psum x1 -> x0, blocking collectives: 39.9 us -> none  [shards(): sq = lax.psum(jnp.sum(grad_part * grad_part), ('shard', 'tensor'))]
    all_gather x1 -> x0, blocking collectives: 32 us -> none  [shards(): lax.all_gather(new_master.astype(jnp.bfloat16), 'shard', axis=0, tiled=True)]
    unnamed x11 -> x15, local copies, waits for them, and re-layouts: 0.9 us -> 9.18 us
    reduce_sum x2 -> x0, other arithmetic: 5.33 us -> none  [the longest x1 3.75 us: shards(): summed = jnp.sum(local.astype(jnp.float32), axis=0)]
    convert_element_type x1 -> x0, other arithmetic: 1.82 us -> none  [shards(): new_master.astype(jnp.bfloat16)]
  transfers between devices with their start and end apart: 1 -> 0, of which waited for: 1 -> 0; matrix products, arithmetic and copies ran while one was open for 0% -> 0% of each run, Pallas kernels for 0% -> 0%
where the time goes in v1:
time: 53.8 us; the launch traced here: 53.5 us
  Pallas kernels  43.7 us (81%)
  local copies, waits for them, and re-layouts  9.18 us (17%)
  between operations  0.66 us (1%)
    pallas_call x1, Pallas kernels, fused(): pl.pallas_call(make_kernel(n_tensor, micro, rows, cols), out_shape=(f32,...  43.7 us
    unnamed x15, local copies, waits for them, and re-layouts  9.18 us

profile of v1, /device:TPU:0, one launch (start us, length us, event | category | flops | bytes accessed | tf_op | source)
XLA Modules:
  0.0 53.5 jit_solution(7839518797055788870)
XLA Ops:
  0.6 0.0 copy-start
  0.6 1.9 %copy-done = bf16[1,4,1536,256]{3,2,1,0:T(8,128)(2,1)S(1)} copy-done((bf16[1,4,1536,256]{3,2,1,0:T(8,128)(2,1)S(1)}, bf16[1,4,1536,256]{3,2,1,0:T(8,128)(2,1)}, u32[]{:S(2)}) %copy-start) | copy-done | bytes 3145752
  2.5 0.0 copy-start.1
  2.5 0.9 %copy-done.1 = f32[192,256]{1,0:T(8,128)S(1)} copy-done((f32[192,256]{1,0:T(8,128)S(1)}, f32[192,256]{1,0:T(8,128)}, u32[]{:S(2)}) %copy-start.1) | copy-done | bytes 196632
  3.5 0.0 copy-start.2
  3.5 0.9 %copy-done.2 = f32[192,256]{1,0:T(8,128)S(1)} copy-done((f32[192,256]{1,0:T(8,128)S(1)}, f32[192,256]{1,0:T(8,128)}, u32[]{:S(2)}) %copy-start.2) | copy-done | bytes 196632
  4.4 0.0 copy-start.3
  4.4 0.9 %copy-done.3 = f32[192,256]{1,0:T(8,128)S(1)} copy-done((f32[192,256]{1,0:T(8,128)S(1)}, f32[192,256]{1,0:T(8,128)}, u32[]{:S(2)}) %copy-start.3) | copy-done | bytes 196632
  5.3 0.0 copy-start.4
  5.3 0.9 %copy-done.4 = f32[192,256]{1,0:T(8,128)S(1)} copy-done((f32[192,256]{1,0:T(8,128)S(1)}, f32[192,256]{1,0:T(8,128)}, u32[]{:S(2)}) %copy-start.4) | copy-done | bytes 196632
  6.2 43.7 %shard_map.92 = (f32[192,256]{1,0:T(8,128)S(1)}, f32[192,256]{1,0:T(8,128)S(1)}, f32[192,256]{1,0:T(8,128)S(1)}, f32[192,256]{1,0:T(8,128)S(1)}, bf16[1536,256]{1,0:T(8,128)(2,1)S(1)}) custom-call(bf16[1,4,1536,256]{3,2,1,0:T(8,128)(2,1)S(1)} %copy-done, f32[192,256]{1,0:T(8,128)S(1)} %copy-done.1, f32[192,256]{1,0:T(8,128)S(1)} %copy-done.2, ...), custom_call_target="tpu_custom_call" | custom-call | flops 20000000 | bytes 6000000 | tf_op jit(solution)/shard_map/pallas_call | solution.py:284
  50.0 0.7 %copy.15 = f32[192,256]{1,0:T(8,128)} copy(f32[192,256]{1,0:T(8,128)S(1)} %get-tuple-element.10) | data formatting | bytes 393216
  50.6 0.7 %copy.16 = f32[192,256]{1,0:T(8,128)} copy(f32[192,256]{1,0:T(8,128)S(1)} %get-tuple-element.11) | data formatting | bytes 393216
  51.3 0.7 %copy.17 = f32[192,256]{1,0:T(8,128)} copy(f32[192,256]{1,0:T(8,128)S(1)} %get-tuple-element.12) | data formatting | bytes 393216
  52.0 0.7 %copy.18 = f32[192,256]{1,0:T(8,128)} copy(f32[192,256]{1,0:T(8,128)S(1)} %get-tuple-element.13) | data formatting | bytes 393216
  52.7 0.9 %copy.19 = bf16[1536,256]{1,0:T(8,128)(2,1)} copy(bf16[1536,256]{1,0:T(8,128)(2,1)S(1)} %get-tuple-element.14) | data formatting | bytes 1572864
Async XLA Ops:
  0.6 1.9 %copy-start = (bf16[1,4,1536,256]{3,2,1,0:T(8,128)(2,1)S(1)}, bf16[1,4,1536,256]{3,2,1,0:T(8,128)(2,1)}, u32[]{:S(2)}) copy-start(bf16[1,4,1536,256]{3,2,1,0:T(8,128)(2,1)} %g.1) | copy-start | bytes 9437188
  2.5 0.9 %copy-start.1 = (f32[192,256]{1,0:T(8,128)S(1)}, f32[192,256]{1,0:T(8,128)}, u32[]{:S(2)}) copy-start(f32[192,256]{1,0:T(8,128)} %ma.1) | copy-start | bytes 589828
  3.5 0.9 %copy-start.2 = (f32[192,256]{1,0:T(8,128)S(1)}, f32[192,256]{1,0:T(8,128)}, u32[]{:S(2)}) copy-start(f32[192,256]{1,0:T(8,128)} %m1.1) | copy-start | bytes 589828
  4.4 0.9 %copy-start.3 = (f32[192,256]{1,0:T(8,128)S(1)}, f32[192,256]{1,0:T(8,128)}, u32[]{:S(2)}) copy-start(f32[192,256]{1,0:T(8,128)} %m2.1) | copy-start | bytes 589828
  5.3 0.9 %copy-start.4 = (f32[192,256]{1,0:T(8,128)S(1)}, f32[192,256]{1,0:T(8,128)}, u32[]{:S(2)}) copy-start(f32[192,256]{1,0:T(8,128)} %em.1) | copy-start | bytes 589828

commit v2 on v0

--- a/solution.py
+++ b/solution.py
@@ -1,10 +1,11 @@
 import jax
 import jax.numpy as jnp
 from jax import lax
+from jax.experimental import pallas as pl
+from jax.experimental.pallas import tpu as pltpu
 from jax.sharding import PartitionSpec as P
 
 STEP = 10
-
 
 beta_one = 0.9
 beta_two = 0.95
@@ -12,8 +13,31 @@
 decay_weight = 0.1
 ema_keep = 0.99
 
-
-def shards(grads, master, moment1, moment2, ema):
+MESH = pl.DeviceIdType.MESH
+TILE = 32
+PIECES = 2
+
+GAIN = 16.0
+LINEAR = 2.0**-12
+
+
+def encode(value):
+    u = jnp.abs(value) * GAIN
+    u2 = u * u
+    u4 = u2 * u2
+    power = jnp.where(u < LINEAR, u * LINEAR**7, u4 * u4)
+    return jnp.where(value < 0, -power, power).astype(jnp.bfloat16)
+
+
+def decode(code):
+    y = code.astype(jnp.float32)
+    a = jnp.abs(y)
+    fourth = lax.rsqrt(lax.rsqrt(a))
+    root = jnp.where(a < LINEAR**8, a * (LINEAR**-7 / GAIN), fourth * lax.rsqrt(fourth) * (1.0 / GAIN))
+    return jnp.where(y < 0, -root, root)
+
+
+def plain(grads, master, moment1, moment2, ema):
     local = grads[0]
     elements = local.shape[1] * local.shape[2] * lax.axis_size("tensor")
     summed = jnp.sum(local.astype(jnp.float32), axis=0)
@@ -33,7 +57,270 @@
     return (new_master, new_moment1, new_moment2, new_ema, weights)
 
 
+def update(clipped, master, moment1, moment2):
+    new_moment1 = beta_one * moment1 + (1.0 - beta_one) * clipped
+    new_moment2 = beta_two * moment2 + (1.0 - beta_two) * clipped * clipped
+    first_hat = new_moment1 / (1.0 - beta_one**STEP)
+    second_hat = new_moment2 / (1.0 - beta_two**STEP)
+    new_master = master - learn_rate * (
+        first_hat / (jnp.sqrt(second_hat) + 1e-08) + decay_weight * master
+    )
+    return new_master, new_moment1, new_moment2
+
+
+def make_kernel(n_tensor, micro, rows, cols):
+    n_shard = 8
+    devices = n_shard * n_tensor
+    elements = n_shard * rows * cols * n_tensor
+    piece = rows // PIECES
+
+    def kernel(g, ma, m1, m2, o_clip, o_w,
+               gv, st, part, sx, rx, sz, rz, w, sq_a,
+               load_sem, store_sem, send_sem, recv_sem, sqs_sem, sqr_sem):
+        s = lax.axis_index("shard")
+        t = lax.axis_index("tensor")
+        me = s * n_tensor + t
+        x = lax.rem(s, 2)
+        z = s // 2
+        other = 1 - x
+        zs = (z, z + 1 - 2 * lax.rem(z, 2), lax.rem(z + 2, 4), 3 - z)
+        to_x = {"shard": 2 * z + other}
+        to_z = {1: {"shard": 2 * zs[1] + x}, 2: {"shard": 2 * zs[2] + x}}
+
+        def block(j, xx):
+            return pl.ds(pl.multiple_of((2 * zs[j] + xx) * rows, rows), rows)
+
+        loads = {}
+        for i, (j, mine) in enumerate(((3, False), (2, False), (3, True), (1, False), (0, False),
+                                       (2, True), (1, True), (0, True))):
+            loads[j, mine] = (i, pltpu.make_async_copy(
+                g.at[0, :, block(j, x if mine else other), :], gv.at[i], load_sem.at[i]))
+            loads[j, mine][1].start()
+        state = []
+        for i, ref in enumerate((ma, m1, m2)):
+            state.append(pltpu.make_async_copy(ref, st.at[i], load_sem.at[8 + i]))
+            state[-1].start()
+
+        def peer(k):
+            index = lax.rem(me + k, devices)
+            return {"shard": index // n_tensor, "tensor": lax.rem(index, n_tensor)}
+
+        barrier = pltpu.get_barrier_semaphore()
+        for k in range(1, devices):
+            pl.semaphore_signal(barrier, inc=1, device_id=peer(k), device_id_type=MESH)
+
+        def tiles(body, h, init=0):
+            def step(i, carry):
+                return body(pl.ds(pl.multiple_of(h * piece + i * TILE, TILE), TILE), carry)
+            return lax.fori_loop(0, piece // TILE, step, init, unroll=True)
+
+        def micro_sum(slot, r):
+            total = gv[slot, 0, r, :].astype(jnp.float32)
+            for m in range(1, micro):
+                total = total + gv[slot, m, r, :].astype(jnp.float32)
+            return total
+
+        sent = []
+
+        def send(src, dst, index, h, target):
+            span = pl.ds(h * piece, piece)
+            copy = pltpu.make_async_remote_copy(
+                src_ref=src.at[span], dst_ref=dst.at[span],
+                send_sem=send_sem.at[index, h], recv_sem=recv_sem.at[index, h],
+                device_id=target, device_id_type=MESH)
+            copy.start()
+            sent.append(copy)
+            return copy
+
+        over_x = {}
+
+        def give(j):
+            slot, copy = loads[j, False]
+            copy.wait()
+            for h in range(PIECES):
+                def body(r, c):
+                    sx[j, r, :] = encode(micro_sum(slot, r))
+                    return c
+                tiles(body, h)
+                if not over_x:
+                    pl.semaphore_wait(barrier, devices - 1)
+                over_x[j, h] = send(sx.at[j], rx.at[j], j, h, to_x)
+
+        def keep(j):
+            slot, copy = loads[j, True]
+            copy.wait()
+
+            def body(r, c):
+                part[j, r, :] = micro_sum(slot, r)
+                return c
+            for h in range(PIECES):
+                tiles(body, h)
+
+        give(3)
+        give(2)
+        keep(3)
+        give(1)
+        give(0)
+        keep(2)
+        keep(1)
+        keep(0)
+
+        first, far, near = [], [], []
+        for h in range(PIECES):
+            over_x[3, h].wait_recv()
+
+            def body(r, c):
+                sz[0, r, :] = encode(part[3, r, :] + decode(rx[3, r, :]))
+                return c
+            tiles(body, h)
+            first.append(send(sz.at[0], rz.at[0], 4, h, to_z[1]))
+        for h in range(PIECES):
+            over_x[2, h].wait_recv()
+            first[h].wait_recv()
+
+            def body(r, c):
+                sz[1, r, :] = encode(part[2, r, :] + decode(rx[2, r, :]) + decode(rz[0, r, :]))
+                return c
+            tiles(body, h)
+            far.append(send(sz.at[1], rz.at[1], 5, h, to_z[2]))
+        for h in range(PIECES):
+            over_x[1, h].wait_recv()
+
+            def body(r, c):
+                sz[2, r, :] = encode(part[1, r, :] + decode(rx[1, r, :]))
+                return c
+            tiles(body, h)
+            near.append(send(sz.at[2], rz.at[2], 6, h, to_z[1]))
+
+        acc = jnp.zeros((8, cols // 2), jnp.float32)
+        for h in range(PIECES):
+            over_x[0, h].wait_recv()
+            near[h].wait_recv()
+            far[h].wait_recv()
+
+            def body(r, acc):
+                total = part[0, r, :] + decode(rx[0, r, :]) + decode(rz[2, r, :]) + decode(rz[1, r, :])
+                part[0, r, :] = total
+                square = total * total
+                square = square[:, :cols // 2] + square[:, cols // 2:]
+                return acc + jnp.sum(square.reshape(TILE // 8, 8, cols // 2), axis=0)
+            acc = tiles(body, h, acc)
+
+        sq_a[me] = jnp.sum(acc, axis=0, keepdims=True)
+        for k in range(1, devices):
+            pltpu.make_async_remote_copy(
+                src_ref=sq_a.at[me], dst_ref=sq_a.at[me], send_sem=sqs_sem, recv_sem=sqr_sem,
+                device_id=peer(k), device_id_type=MESH).start()
+        for copy in state:
+            copy.wait()
+        others = sq_a.at[pl.ds(0, devices - 1)]
+        pltpu.make_async_copy(others, others, sqr_sem).wait()
+        sq = jnp.sum(jnp.sum(sq_a[...], axis=0), axis=1, keepdims=True)
+        scale = jnp.minimum(1.0, 1.0 / jnp.sqrt(sq / elements + 1e-06))
+
+        def gathered(slot, index, h, target):
+            return send(w.at[slot], w.at[slot], index, h, target)
+
+        slot_x = [2 * zj + x for zj in zs]
+        slot_o = [2 * zj + other for zj in zs]
+        stores = []
+
+        def store(src, dst):
+            copy = pltpu.make_async_copy(src, dst, store_sem.at[len(stores)])
+            copy.start()
+            stores.append(copy)
+
+        def store_w(slot, h):
+            store(w.at[slot, pl.ds(h * piece, piece)],
+                  o_w.at[pl.ds(pl.multiple_of(slot * rows + h * piece, piece), piece), :])
+
+        far, near, side = [], [], []
+        for h in range(PIECES):
+            def body(r, c):
+                clipped = scale * part[0, r, :]
+                part[0, r, :] = clipped
+                w[s, r, :] = update(clipped, st[0, r, :], st[1, r, :], st[2, r, :])[0].astype(jnp.bfloat16)
+                return c
+            tiles(body, h)
+            far.append(gathered(s, 9, h, to_z[2]))
+            near.append(gathered(s, 8, h, to_z[1]))
+            side.append(gathered(s, 7, h, to_x))
+            store_w(s, h)
+        store(part.at[0], o_clip)
+
+        near_2, ends = [], []
+        for h in range(PIECES):
+            near[h].wait_recv()
+            ends.append((gathered(slot_x[1], 11, h, to_x), 1, h))
+            store_w(slot_x[1], h)
+            far[h].wait_recv()
+            near_2.append(gathered(slot_x[2], 10, h, to_z[1]))
+            ends.append((gathered(slot_x[2], 12, h, to_x), 2, h))
+            store_w(slot_x[2], h)
+        for h in range(PIECES):
+            side[h].wait_recv()
+            store_w(slot_o[0], h)
+        for h in range(PIECES):
+            near_2[h].wait_recv()
+            ends.append((gathered(slot_x[3], 13, h, to_x), 3, h))
+            store_w(slot_x[3], h)
+        for copy, j, h in ends:
+            copy.wait_recv()
+            store_w(slot_o[j], h)
+        for copy in sent:
+            copy.wait_send()
+        pltpu.make_async_copy(others, others, sqs_sem).wait()
+        for copy in stores:
+            copy.wait()
+
+    return kernel
+
+
+def fused(grads, master, moment1, moment2, ema):
+    n_tensor = lax.axis_size("tensor")
+    micro = grads.shape[1]
+    rows, cols = master.shape
+    f32 = jax.ShapeDtypeStruct((rows, cols), jnp.float32)
+    full = jax.ShapeDtypeStruct((8 * rows, cols), jnp.bfloat16)
+    anywhere = pl.BlockSpec(memory_space=pl.ANY)
+    clipped, weights = pl.pallas_call(
+        make_kernel(n_tensor, micro, rows, cols),
+        out_shape=(f32, full),
+        in_specs=[anywhere] * 4,
+        out_specs=(anywhere,) * 2,
+        scratch_shapes=[
+            pltpu.VMEM((8, micro, rows, cols), jnp.bfloat16),
+            pltpu.VMEM((3, rows, cols), jnp.float32),
+            pltpu.VMEM((4, rows, cols), jnp.float32),
+            pltpu.VMEM((4, rows, cols), jnp.bfloat16),
+            pltpu.VMEM((4, rows, cols), jnp.bfloat16),
+            pltpu.VMEM((3, rows, cols), jnp.bfloat16),
+            pltpu.VMEM((3, rows, cols), jnp.bfloat16),
+            pltpu.VMEM((8, rows, cols), jnp.bfloat16),
+            pltpu.VMEM((8 * n_tensor, 1, cols // 2), jnp.float32),
+            pltpu.SemaphoreType.DMA((11,)),
+            pltpu.SemaphoreType.DMA((8 * PIECES + 1,)),
+            pltpu.SemaphoreType.DMA((14, PIECES)),
+            pltpu.SemaphoreType.DMA((14, PIECES)),
+            pltpu.SemaphoreType.DMA,
+            pltpu.SemaphoreType.DMA,
+        ],
+        compiler_params=pltpu.CompilerParams(
+            collective_id=0, has_side_effects=True, vmem_limit_bytes=64 * 1024 * 1024
+        ),
+        cost_estimate=pl.CostEstimate(flops=20_000_000, bytes_accessed=6_000_000, transcendentals=300_000),
+    )(grads, master, moment1, moment2)
+    new_master, new_moment1, new_moment2 = update(clipped, master, moment1, moment2)
+    new_ema = ema_keep * ema + (1.0 - ema_keep) * new_master
+    return (new_master, new_moment1, new_moment2, new_ema, weights)
+
+
 def solution(mesh):
+    def shards(grads, master, moment1, moment2, ema):
+        if mesh.shape["shard"] == 8 and master.shape[0] % (PIECES * TILE) == 0 and master.shape[1] == 256:
+            return fused(grads, master, moment1, moment2, ema)
+        return plain(grads, master, moment1, moment2, ema)
+
     return jax.shard_map(
         shards,
         mesh=mesh,

time: 164 us -> 42.3 us (0.26)
  blocking collectives: 71.9 us -> 0 us
  waiting for transfers between devices: 68 us -> 0 us
  Pallas kernels: 0 us -> 37.2 us
  between operations: 14.8 us -> 0.64 us
  other arithmetic: 7.86 us -> 2.26 us
    reduce_scatter x1 -> x0, waiting for transfers between devices: 67.9 us -> none  [shards(): lax.psum_scatter(summed, 'shard', scatter_dimension=0, tiled=True)]
    psum x1 -> x0, blocking collectives: 39.9 us -> none  [shards(): sq = lax.psum(jnp.sum(grad_part * grad_part), ('shard', 'tensor'))]
    pallas_call x0 -> x1, Pallas kernels: none -> 37.2 us  [fused(): pl.pallas_call(make_kernel(n_tensor, micro, rows, cols), out_shape=(f32,...]
    all_gather x1 -> x0, blocking collectives: 32 us -> none  [shards(): lax.all_gather(new_master.astype(jnp.bfloat16), 'shard', axis=0, tiled=True)]
    reduce_sum x2 -> x0, other arithmetic: 5.33 us -> none  [the longest x1 3.75 us: shards(): summed = jnp.sum(local.astype(jnp.float32), axis=0)]
    convert_element_type x1 -> x0, other arithmetic: 1.82 us -> none  [shards(): new_master.astype(jnp.bfloat16)]
  transfers between devices with their start and end apart: 1 -> 0, of which waited for: 1 -> 0; matrix products, arithmetic and copies ran while one was open for 0% -> 0% of each run, Pallas kernels for 0% -> 0%
where the time goes in v2:
time: 42.3 us; the launch traced here: 42.2 us
  Pallas kernels  37.2 us (88%)
  other arithmetic  2.26 us (5%)
  local copies, waits for them, and re-layouts  2.06 us (5%)
  between operations  0.64 us (2%)
    pallas_call x1, Pallas kernels, fused(): pl.pallas_call(make_kernel(n_tensor, micro, rows, cols), out_shape=(f32,...  37.2 us
    add x1, other arithmetic, fused(): new_ema = ema_keep * ema + (1.0 - ema_keep) * new_master  2.26 us
    unnamed x1, local copies, waits for them, and re-layouts  2.06 us

profile of v2, /device:TPU:0, one launch (start us, length us, event | category | flops | bytes accessed | tf_op | source)
XLA Modules:
  0.0 42.2 jit_solution(2775228628419171894)
XLA Ops:
  0.6 37.2 %shard_map.92 = (f32[192,256]{1,0:T(8,128)}, bf16[1536,256]{1,0:T(8,128)(2,1)}) custom-call(bf16[1,4,1536,256]{3,2,1,0:T(8,128)(2,1)} %g.1, f32[192,256]{1,0:T(8,128)} %ma.1, f32[192,256]{1,0:T(8,128)} %m1.1, f32[192,256]{1,0:T(8,128)} %m2.1), custom_call_target="tpu_custom_call" | custom-call | flops 20000000 | bytes 6000000 | tf_op jit(solution)/shard_map/pallas_call | solution.py:286
  37.8 2.3 %multiply_add_fusion = (f32[192,256]{1,0:T(8,128)}, f32[192,256]{1,0:T(8,128)}, f32[192,256]{1,0:T(8,128)}, f32[192,256]{1,0:T(8,128)}) fusion(f32[192,256]{1,0:T(8,128)} %param.9, f32[192,256]{1,0:T(8,128)} %ma.1, f32[192,256]{1,0:T(8,128)} %get-tuple-element.7, f32[192,256]{1,0:T(8,128)} %m1.1, f32[192,256]{1,0:T(8,128)} %m2.1), kind=kLoop, calls=%fused_computation.2 | loop fusion | flops 884736 | bytes 1769472 | tf_op jit(solution)/shard_map/add | solution.py:314
  40.1 2.1 %copy.11 = bf16[1536,256]{1,0:T(8,128)(2,1)} copy(bf16[1536,256]{1,0:T(8,128)(2,1)} %get-tuple-element.22) | data formatting | bytes 1572864

commit v3 on v2

--- a/solution.py
+++ b/solution.py
@@ -16,6 +16,7 @@
 MESH = pl.DeviceIdType.MESH
 TILE = 32
 PIECES = 2
+LAST = PIECES - 1
 
 GAIN = 16.0
 LINEAR = 2.0**-12
@@ -74,9 +75,9 @@
     elements = n_shard * rows * cols * n_tensor
     piece = rows // PIECES
 
-    def kernel(g, ma, m1, m2, o_clip, o_w,
-               gv, st, part, sx, rx, sz, rz, w, sq_a,
-               load_sem, store_sem, send_sem, recv_sem, sqs_sem, sqr_sem):
+    def kernel(g, ma, m1, m2, o_clip, w,
+               gv, st, part, sx, rx, sz, rz, sq_a,
+               load_sem, send_sem, recv_sem, sqs_sem, sqr_sem):
         s = lax.axis_index("shard")
         t = lax.axis_index("tensor")
         me = s * n_tensor + t
@@ -91,7 +92,7 @@
             return pl.ds(pl.multiple_of((2 * zs[j] + xx) * rows, rows), rows)
 
         loads = {}
-        for i, (j, mine) in enumerate(((3, False), (2, False), (3, True), (1, False), (0, False),
+        for i, (j, mine) in enumerate(((3, False), (1, False), (2, False), (3, True), (0, False),
                                        (2, True), (1, True), (0, True))):
             loads[j, mine] = (i, pltpu.make_async_copy(
                 g.at[0, :, block(j, x if mine else other), :], gv.at[i], load_sem.at[i]))
@@ -134,17 +135,27 @@
 
         over_x = {}
 
-        def give(j):
+        def give(j, pieces=range(PIECES)):
             slot, copy = loads[j, False]
-            copy.wait()
-            for h in range(PIECES):
+            if j != 1 or LAST in pieces:
+                copy.wait()
+            for h in pieces:
+                if (j, h) == (0, LAST):
+                    over_x[1, LAST].wait_recv()
+
                 def body(r, c):
-                    sx[j, r, :] = encode(micro_sum(slot, r))
+                    total = micro_sum(slot, r)
+                    if (j, h) == (0, LAST):
+                        total = total + decode(rz[3, r, :])
+                    sx[j, r, :] = encode(total)
                     return c
                 tiles(body, h)
                 if not over_x:
                     pl.semaphore_wait(barrier, devices - 1)
-                over_x[j, h] = send(sx.at[j], rx.at[j], j, h, to_x)
+                if (j, h) == (1, LAST):
+                    over_x[j, h] = send(sx.at[j], rz.at[3], 14, h, to_z[1])
+                else:
+                    over_x[j, h] = send(sx.at[j], rx.at[j], j, h, to_x)
 
         def keep(j):
             slot, copy = loads[j, True]
@@ -157,13 +168,14 @@
                 tiles(body, h)
 
         give(3)
+        give(1, (LAST,))
         give(2)
         keep(3)
-        give(1)
-        give(0)
+        give(1, range(LAST))
         keep(2)
         keep(1)
         keep(0)
+        give(0)
 
         first, far, near = [], [], []
         for h in range(PIECES):
@@ -184,10 +196,14 @@
             tiles(body, h)
             far.append(send(sz.at[1], rz.at[1], 5, h, to_z[2]))
         for h in range(PIECES):
-            over_x[1, h].wait_recv()
-
-            def body(r, c):
-                sz[2, r, :] = encode(part[1, r, :] + decode(rx[1, r, :]))
+            if h != LAST:
+                over_x[1, h].wait_recv()
+
+            def body(r, c):
+                total = part[1, r, :]
+                if h != LAST:
+                    total = total + decode(rx[1, r, :])
+                sz[2, r, :] = encode(total)
                 return c
             tiles(body, h)
             near.append(send(sz.at[2], rz.at[2], 6, h, to_z[1]))
@@ -223,55 +239,39 @@
 
         slot_x = [2 * zj + x for zj in zs]
         slot_o = [2 * zj + other for zj in zs]
-        stores = []
-
-        def store(src, dst):
-            copy = pltpu.make_async_copy(src, dst, store_sem.at[len(stores)])
-            copy.start()
-            stores.append(copy)
-
-        def store_w(slot, h):
-            store(w.at[slot, pl.ds(h * piece, piece)],
-                  o_w.at[pl.ds(pl.multiple_of(slot * rows + h * piece, piece), piece), :])
-
         far, near, side = [], [], []
         for h in range(PIECES):
             def body(r, c):
                 clipped = scale * part[0, r, :]
-                part[0, r, :] = clipped
+                o_clip[r, :] = clipped
                 w[s, r, :] = update(clipped, st[0, r, :], st[1, r, :], st[2, r, :])[0].astype(jnp.bfloat16)
                 return c
             tiles(body, h)
             far.append(gathered(s, 9, h, to_z[2]))
             near.append(gathered(s, 8, h, to_z[1]))
             side.append(gathered(s, 7, h, to_x))
-            store_w(s, h)
-        store(part.at[0], o_clip)
 
         near_2, ends = [], []
         for h in range(PIECES):
             near[h].wait_recv()
-            ends.append((gathered(slot_x[1], 11, h, to_x), 1, h))
-            store_w(slot_x[1], h)
+            if h != LAST:
+                ends.append((gathered(slot_x[1], 11, h, to_x), 1, h))
             far[h].wait_recv()
             near_2.append(gathered(slot_x[2], 10, h, to_z[1]))
             ends.append((gathered(slot_x[2], 12, h, to_x), 2, h))
-            store_w(slot_x[2], h)
-        for h in range(PIECES):
+            if h == 0:
+                side[LAST].wait_recv()
+                ends.append((gathered(slot_o[0], 11, LAST, to_z[1]), 1, LAST))
+        for h in range(LAST):
             side[h].wait_recv()
-            store_w(slot_o[0], h)
         for h in range(PIECES):
             near_2[h].wait_recv()
             ends.append((gathered(slot_x[3], 13, h, to_x), 3, h))
-            store_w(slot_x[3], h)
         for copy, j, h in ends:
             copy.wait_recv()
-            store_w(slot_o[j], h)
         for copy in sent:
             copy.wait_send()
         pltpu.make_async_copy(others, others, sqs_sem).wait()
-        for copy in stores:
-            copy.wait()
 
     return kernel
 
@@ -281,13 +281,13 @@
     micro = grads.shape[1]
     rows, cols = master.shape
     f32 = jax.ShapeDtypeStruct((rows, cols), jnp.float32)
-    full = jax.ShapeDtypeStruct((8 * rows, cols), jnp.bfloat16)
+    full = jax.ShapeDtypeStruct((8, rows, cols), jnp.bfloat16)
     anywhere = pl.BlockSpec(memory_space=pl.ANY)
     clipped, weights = pl.pallas_call(
         make_kernel(n_tensor, micro, rows, cols),
-        out_shape=(f32, full),
+        out_shape=(pltpu.VMEM(f32.shape, f32.dtype), pltpu.VMEM(full.shape, full.dtype)),
         in_specs=[anywhere] * 4,
-        out_specs=(anywhere,) * 2,
+        out_specs=(pl.BlockSpec(memory_space=pltpu.VMEM),) * 2,
         scratch_shapes=[
             pltpu.VMEM((8, micro, rows, cols), jnp.bfloat16),
             pltpu.VMEM((3, rows, cols), jnp.float32),
@@ -295,24 +295,22 @@
             pltpu.VMEM((4, rows, cols), jnp.bfloat16),
             pltpu.VMEM((4, rows, cols), jnp.bfloat16),
             pltpu.VMEM((3, rows, cols), jnp.bfloat16),
-            pltpu.VMEM((3, rows, cols), jnp.bfloat16),
-            pltpu.VMEM((8, rows, cols), jnp.bfloat16),
+            pltpu.VMEM((4, rows, cols), jnp.bfloat16),
             pltpu.VMEM((8 * n_tensor, 1, cols // 2), jnp.float32),
             pltpu.SemaphoreType.DMA((11,)),
-            pltpu.SemaphoreType.DMA((8 * PIECES + 1,)),
-            pltpu.SemaphoreType.DMA((14, PIECES)),
-            pltpu.SemaphoreType.DMA((14, PIECES)),
+            pltpu.SemaphoreType.DMA((15, PIECES)),
+            pltpu.SemaphoreType.DMA((15, PIECES)),
             pltpu.SemaphoreType.DMA,
             pltpu.SemaphoreType.DMA,
         ],
         compiler_params=pltpu.CompilerParams(
-            collective_id=0, has_side_effects=True, vmem_limit_bytes=64 * 1024 * 1024
+            collective_id=0, has_side_effects=True, vmem_limit_bytes=63 * 1024 * 1024
         ),
         cost_estimate=pl.CostEstimate(flops=20_000_000, bytes_accessed=6_000_000, transcendentals=300_000),
     )(grads, master, moment1, moment2)
     new_master, new_moment1, new_moment2 = update(clipped, master, moment1, moment2)
     new_ema = ema_keep * ema + (1.0 - ema_keep) * new_master
-    return (new_master, new_moment1, new_moment2, new_ema, weights)
+    return (new_master, new_moment1, new_moment2, new_ema, weights.reshape(8 * rows, cols))
 
 
 def solution(mesh):

time: 42.3 us -> 40.9 us (0.967)
  local copies, waits for them, and re-layouts: 2.06 us -> 0.88 us
    unnamed x1, local copies, waits for them, and re-layouts: 2.06 us -> 0.88 us
where the time goes in v3:
time: 40.9 us; the launch traced here: 40.8 us
  Pallas kernels  37.1 us (91%)
  other arithmetic  2.2 us (5%)
  local copies, waits for them, and re-layouts  0.88 us (2%)
  between operations  0.64 us (2%)
    pallas_call x1, Pallas kernels, fused(): pl.pallas_call(make_kernel(n_tensor, micro, rows, cols), out_shape=(pltpu...  37.1 us
    add x1, other arithmetic, fused(): new_ema = ema_keep * ema + (1.0 - ema_keep) * new_master  2.2 us
    unnamed x1, local copies, waits for them, and re-layouts  0.88 us

profile of v3, /device:TPU:0, one launch (start us, length us, event | category | flops | bytes accessed | tf_op | source)
XLA Modules:
  0.0 40.8 jit_solution(7849313037277671141)
XLA Ops:
  0.6 37.1 %shard_map.92 = (f32[192,256]{1,0:T(8,128)S(1)}, bf16[8,192,256]{2,1,0:T(8,128)(2,1)S(1)}) custom-call(bf16[1,4,1536,256]{3,2,1,0:T(8,128)(2,1)} %g.1, f32[192,256]{1,0:T(8,128)} %ma.1, f32[192,256]{1,0:T(8,128)} %m1.1, f32[192,256]{1,0:T(8,128)} %m2.1), custom_call_target="tpu_custom_call" | custom-call | flops 20000000 | bytes 6000000 | tf_op jit(solution)/shard_map/pallas_call | solution.py:286
  37.7 0.9 %copy.11 = bf16[1536,256]{1,0:T(8,128)(2,1)} copy(bf16[1536,256]{1,0:T(8,128)(2,1)S(1)} %bitcast.1) | data formatting | bytes 1572864
  38.6 2.2 %multiply_add_fusion = (f32[192,256]{1,0:T(8,128)}, f32[192,256]{1,0:T(8,128)}, f32[192,256]{1,0:T(8,128)}, f32[192,256]{1,0:T(8,128)}) fusion(f32[192,256]{1,0:T(8,128)} %param.9, f32[192,256]{1,0:T(8,128)} %ma.1, f32[192,256]{1,0:T(8,128)S(1)} %get-tuple-element.7, f32[192,256]{1,0:T(8,128)} %m1.1, f32[192,256]{1,0:T(8,128)} %m2.1), kind=kLoop, calls=%fused_computation.2 | loop fusion | flops 884736 | bytes 1769472 | tf_op jit(solution)/shard_map/add | solution.py:312

commit v4 on v3

--- a/solution.py
+++ b/solution.py
@@ -15,7 +15,7 @@
 
 MESH = pl.DeviceIdType.MESH
 TILE = 32
-PIECES = 2
+PIECES = 3
 LAST = PIECES - 1
 
 GAIN = 16.0
@@ -75,7 +75,7 @@
     elements = n_shard * rows * cols * n_tensor
     piece = rows // PIECES
 
-    def kernel(g, ma, m1, m2, o_clip, w,
+    def kernel(g, ma, m1, m2, em, o_ma, o_m1, o_m2, o_em, w,
                gv, st, part, sx, rx, sz, rz, sq_a,
                load_sem, send_sem, recv_sem, sqs_sem, sqr_sem):
         s = lax.axis_index("shard")
@@ -98,7 +98,7 @@
                 g.at[0, :, block(j, x if mine else other), :], gv.at[i], load_sem.at[i]))
             loads[j, mine][1].start()
         state = []
-        for i, ref in enumerate((ma, m1, m2)):
+        for i, ref in enumerate((ma, m1, m2, em)):
             state.append(pltpu.make_async_copy(ref, st.at[i], load_sem.at[8 + i]))
             state[-1].start()
 
@@ -243,13 +243,22 @@
         for h in range(PIECES):
             def body(r, c):
                 clipped = scale * part[0, r, :]
-                o_clip[r, :] = clipped
-                w[s, r, :] = update(clipped, st[0, r, :], st[1, r, :], st[2, r, :])[0].astype(jnp.bfloat16)
+                new_ma, new_m1, new_m2 = update(clipped, st[0, r, :], st[1, r, :], st[2, r, :])
+                w[s, r, :] = new_ma.astype(jnp.bfloat16)
+                o_ma[r, :] = new_ma
+                o_m1[r, :] = new_m1
+                o_m2[r, :] = new_m2
                 return c
             tiles(body, h)
             far.append(gathered(s, 9, h, to_z[2]))
             near.append(gathered(s, 8, h, to_z[1]))
             side.append(gathered(s, 7, h, to_x))
+
+        def body(r, c):
+            o_em[r, :] = ema_keep * st[3, r, :] + (1.0 - ema_keep) * o_ma[r, :]
+            return c
+        for h in range(PIECES):
+            tiles(body, h)
 
         near_2, ends = [], []
         for h in range(PIECES):
@@ -276,6 +285,14 @@
     return kernel
 
 
+def hand_over(*refs):
+    copies = [pltpu.make_async_copy(refs[i], refs[5 + i], refs[10].at[i]) for i in range(5)]
+    for copy in copies:
+        copy.start()
+    for copy in copies:
+        copy.wait()
+
+
 def fused(grads, master, moment1, moment2, ema):
     n_tensor = lax.axis_size("tensor")
     micro = grads.shape[1]
@@ -283,34 +300,42 @@
     f32 = jax.ShapeDtypeStruct((rows, cols), jnp.float32)
     full = jax.ShapeDtypeStruct((8, rows, cols), jnp.bfloat16)
     anywhere = pl.BlockSpec(memory_space=pl.ANY)
-    clipped, weights = pl.pallas_call(
+    inside = pl.BlockSpec(memory_space=pltpu.VMEM)
+    results = pl.pallas_call(
         make_kernel(n_tensor, micro, rows, cols),
-        out_shape=(pltpu.VMEM(f32.shape, f32.dtype), pltpu.VMEM(full.shape, full.dtype)),
-        in_specs=[anywhere] * 4,
-        out_specs=(pl.BlockSpec(memory_space=pltpu.VMEM),) * 2,
+        out_shape=(pltpu.VMEM(f32.shape, f32.dtype),) * 4 + (pltpu.VMEM(full.shape, full.dtype),),
+        in_specs=[anywhere] * 5,
+        out_specs=(inside,) * 5,
         scratch_shapes=[
             pltpu.VMEM((8, micro, rows, cols), jnp.bfloat16),
-            pltpu.VMEM((3, rows, cols), jnp.float32),
+            pltpu.VMEM((4, rows, cols), jnp.float32),
             pltpu.VMEM((4, rows, cols), jnp.float32),
             pltpu.VMEM((4, rows, cols), jnp.bfloat16),
             pltpu.VMEM((4, rows, cols), jnp.bfloat16),
             pltpu.VMEM((3, rows, cols), jnp.bfloat16),
             pltpu.VMEM((4, rows, cols), jnp.bfloat16),
             pltpu.VMEM((8 * n_tensor, 1, cols // 2), jnp.float32),
-            pltpu.SemaphoreType.DMA((11,)),
+            pltpu.SemaphoreType.DMA((12,)),
             pltpu.SemaphoreType.DMA((15, PIECES)),
             pltpu.SemaphoreType.DMA((15, PIECES)),
             pltpu.SemaphoreType.DMA,
             pltpu.SemaphoreType.DMA,
         ],
         compiler_params=pltpu.CompilerParams(
-            collective_id=0, has_side_effects=True, vmem_limit_bytes=63 * 1024 * 1024
+            collective_id=0, has_side_effects=True, vmem_limit_bytes=63936 * 1024
         ),
         cost_estimate=pl.CostEstimate(flops=20_000_000, bytes_accessed=6_000_000, transcendentals=300_000),
-    )(grads, master, moment1, moment2)
-    new_master, new_moment1, new_moment2 = update(clipped, master, moment1, moment2)
-    new_ema = ema_keep * ema + (1.0 - ema_keep) * new_master
-    return (new_master, new_moment1, new_moment2, new_ema, weights.reshape(8 * rows, cols))
+    )(grads, master, moment1, moment2, ema)
+    outputs = pl.pallas_call(
+        hand_over,
+        out_shape=(f32, f32, f32, f32, full),
+        in_specs=[inside] * 5,
+        out_specs=(anywhere,) * 5,
+        scratch_shapes=[pltpu.SemaphoreType.DMA((5,))],
+        compiler_params=pltpu.CompilerParams(vmem_limit_bytes=4 * 1024 * 1024),
+        cost_estimate=pl.CostEstimate(flops=0, bytes_accessed=3_000_000, transcendentals=0),
+    )(*results)
+    return tuple(outputs[:4]) + (outputs[4].reshape(8 * rows, cols),)
 
 
 def solution(mesh):

time: 40.9 us -> 38.4 us (0.939)
  other arithmetic: 2.2 us -> 0 us
  local copies, waits for them, and re-layouts: 0.88 us -> 0 us
  Pallas kernels: 37.1 us -> 37.6 us
    add x1 -> x0, other arithmetic: 2.2 us -> none  [fused(): new_ema = ema_keep * ema + (1.0 - ema_keep) * new_master]
    pallas_call x0 -> x1, Pallas kernels: none -> 1.18 us  [fused(): pl.pallas_call(hand_over, out_shape=(f32, f32, f32, f32, full), in_specs=...]
    unnamed x1 -> x0, local copies, waits for them, and re-layouts: 0.88 us -> none
    pallas_call x1, Pallas kernels: 37.1 us -> 36.5 us  [fused(): pl.pallas_call(make_kernel(n_tensor, micro, rows, cols), out_shape=(pltpu...]
where the time goes in v4:
time: 38.4 us; the launch traced here: 38.3 us
  Pallas kernels  37.6 us (98%)
  between operations  0.64 us (2%)
    pallas_call x1, Pallas kernels, fused(): pl.pallas_call(make_kernel(n_tensor, micro, rows, cols), out_shape=(pltpu...  36.5 us
    pallas_call x1, Pallas kernels, fused(): pl.pallas_call(hand_over, out_shape=(f32, f32, f32, f32, full), in_specs=...  1.18 us

profile of v4, /device:TPU:0, one launch (start us, length us, event | category | flops | bytes accessed | tf_op | source)
XLA Modules:
  0.0 38.3 jit_solution(6226444886584872062)
XLA Ops:
  0.6 36.5 %shard_map.92 = (f32[192,256]{1,0:T(8,128)S(1)}, f32[192,256]{1,0:T(8,128)S(1)}, f32[192,256]{1,0:T(8,128)S(1)}, f32[192,256]{1,0:T(8,128)S(1)}, bf16[8,192,256]{2,1,0:T(8,128)(2,1)S(1)}) custom-call(bf16[1,4,1536,256]{3,2,1,0:T(8,128)(2,1)} %g.1, f32[192,256]{1,0:T(8,128)} %ma.1, f32[192,256]{1,0:T(8,128)} %m1.1, f32[192,256]{1,0:T(8,128)} %m2.1, f32[192,256]{1,0:T(8,128)} %em.1), custom_call_target="tpu_custom_call" | custom-call | flops 20000000 | bytes 6000000 | tf_op jit(solution)/shard_map/pallas_call | solution.py:304
  37.1 1.2 %shard_map.93 = (f32[192,256]{1,0:T(8,128)}, f32[192,256]{1,0:T(8,128)}, f32[192,256]{1,0:T(8,128)}, f32[192,256]{1,0:T(8,128)}, bf16[8,192,256]{2,1,0:T(8,128)(2,1)}) custom-call(f32[192,256]{1,0:T(8,128)S(1)} %get-tuple-element.15.refs_0_, f32[192,256]{1,0:T(8,128)S(1)} %get-tuple-element.16.refs_1_, f32[192,256]{1,0:T(8,128)S(1)} %get-tuple-element.17.refs_2_, ...), custom_call_target="tpu_custom_call" | custom-call | bytes 3000000 | tf_op jit(solution)/shard_map/pallas_call | solution.py:329
